TPU v7x, 32 devices: a whole 2x2x4 slice. The times are simulated.
32 devices in a mesh: seq: 2 (over y), col: 4 (over z), tp: 4 (over x, core).
Axes of the slice: x: 2, y: 2, z: 4, core: 2. Of those that a mesh axis runs over, the one named last changes fastest.
Arguments:
- inputs: bfloat16 [4096, 8192], P(('seq', 'tp'), 'col'), may hold values from -6 to 6
- grads: bfloat16 [4096, 8192], P(('seq', 'tp'), 'col'), may hold values from -0.035888672 to 0.035888672
- h_in: bfloat16 [8192, 8192], P(None, 'col'), may hold values from -0.0625 to 0.0625
- segments: int32 [8, 512], P(('seq', 'tp')), may hold values from 0 to 3, never falling along the last dimension, each value on 1 to 256 neighbouring positions
Outputs:
- h_out: float32 [8192, 8192], P(('seq', 'tp'), 'col')
Inputs may be any that keep to these rules, and one draw needn't show every extreme that they name: `segments`: within each sequence the numbers never fall; every document has 1 to 256 tokens.
All inputs are finite; a program needn't handle non-finite values.
Results may differ from a plain program's by a relative error of at most 0.005.
Values may be sent and summed in bfloat16 or wider, within the bound.
A program may use at most 128 MiB of HBM per device.

v0:
```python
import jax
import jax.numpy as jnp
from jax import lax
from jax.sharding import PartitionSpec as P


def per_device(inputs, grads, h_in, segments):
    x_full = lax.all_gather(inputs, "col", axis=1, tiled=True)
    projected = jnp.dot(x_full, h_in, preferred_element_type=jnp.float32).astype(jnp.bfloat16)
    partials = [
        lax.dot_general(
            projected, inputs, (((1,), (1,)), ((), ())), preferred_element_type=jnp.float32
        )
    ]
    partial_squares = jnp.stack(partials)
    whole_sum = lax.psum(partial_squares, "col")
    same = segments[:, :, None] == segments[:, None, :]
    squares = jnp.where(same, whole_sum, jnp.float32(0.0)).astype(jnp.bfloat16)
    d_full = lax.all_gather(grads, "col", axis=1, tiled=True)
    products = jnp.dot(squares[0], grads, preferred_element_type=jnp.float32).astype(jnp.bfloat16)
    owned_grads = lax.all_to_all(d_full, ("seq", "tp"), split_axis=1, concat_axis=0, tiled=True)
    return lax.dot_general(
        owned_grads,
        lax.all_gather(products, ("seq", "tp"), axis=0, tiled=True),
        (((0,), (0,)), ((), ())),
        preferred_element_type=jnp.float32,
    )


def solution(mesh):
    placed = (
        P(("seq", "tp"), "col"),
        P(("seq", "tp"), "col"),
        P(None, "col"),
        P(("seq", "tp"), None),
    )
    return jax.shard_map(
        per_device, mesh=mesh, in_specs=placed, out_specs=P(("seq", "tp"), "col"), check_vma=False
    )
```

profile of v0, /device:TPU:7, one launch (start us, length us, event | category | flops | bytes accessed | tf_op | source)
XLA Modules:
  0.0 550.5 jit_solution(7444874340461178741)
XLA Ops:
  6.5 0.0 copy-start
  6.5 0.0 all-gather.4.cloned.1.call-start
  6.5 0.7 all-gather.4.cloned.1.call-update
  7.3 0.0 all-gather.8.cloned.1.call-start
  7.3 3.9 copy.7
  11.2 0.0 all-gather.8.cloned.1.call-update
  11.3 0.0 all-gather.6.cloned.1.call-start
  11.3 148.7 %all-gather.4.cloned.1.call-done = bf16[512,8192]{1,0:T(8,128)(2,1)} async-done(((bf16[512,2048]{1,0:T(8,128)(2,1)}), bf16[512,8192]{1,0:T(8,128)(2,1)}) %all-gather.4.cloned.1.call-update) | async-done | bytes 8388624 | tf_op jit(solution)/shard_map/all_gather | solution.py:8
  160.0 0.0 copy-done
  160.0 0.0 copy-start.1
  160.0 24.9 %fusion.1 = f32[1,512,512]{2,1,0:T(8,128)S(1)} fusion(bf16[512,2048]{1,0:T(8,128)(2,1)S(1)} %copy-done, bf16[512,8192]{1,0:T(8,128)(2,1)} %all-gather.4.cloned.1.call-done, bf16[8192,2048]{1,0:T(8,128)(2,1)} %param.6), kind=kOutput, calls=%fused_computation.4 | convolution fusion | flops 18254659584 | bytes 45088768 | tf_op jit(solution)/shard_map/dot_general | solution.py:11
  184.9 75.0 %all-reduce.1 = bf16[1,512,512]{2,1,0:T(8,128)(2,1)S(1)} all-reduce(f32[1,512,512]{2,1,0:T(8,128)S(1)} %fusion.1), channel_id=1, replica_groups=mesh['seq'=2,'col'=4,'tp'=4] {'col'}, use_global_device_ids=true, to_apply=%region_0.0 | all-reduce | flops 262144 | bytes 1572864 | tf_op jit(solution)/shard_map/psum | solution.py:16
  259.9 0.0 copy-done.1
  260.0 4.2 convolution_convert_fusion.1
  264.2 0.0 all-gather.6.cloned.1.call-update
  264.2 78.7 %all-gather.8.cloned.1.call-done = bf16[512,8192]{0,1:T(8,128)(2,1)} async-done(((bf16[512,2048]{0,1:T(8,128)(2,1)}), bf16[512,8192]{0,1:T(8,128)(2,1)}) %all-gather.8.cloned.1.call-update) | async-done | bytes 8388624 | tf_op jit(solution)/shard_map/all_gather | solution.py:19
  343.0 151.6 %all_to_all.19 = bf16[512,8,1024]{0,2,1:T(8,128)(2,1)} all-to-all(bf16[512,8,1024]{0,2,1:T(8,128)(2,1)} %bitcast.18), channel_id=1, replica_groups=mesh['seq'=2,'col'=4,'tp'=4] {'seq','tp'}, dimensions={1} | all-to-all | bytes 16777216 | tf_op jit(solution)/shard_map/all_to_all | solution.py:21
  494.5 11.4 %copy.8 = bf16[8,512,1024]{2,1,0:T(8,128)(2,1)} copy(bf16[8,512,1024]{1,2,0:T(8,128)(2,1)} %bitcast.17) | data formatting | bytes 16777216 | tf_op jit(solution)/shard_map/all_to_all | solution.py:21
  505.9 4.9 all-gather.6.cloned.1.call-done
  510.8 24.1 %convolution_bitcast_fusion = f32[1024,2048]{0,1:T(8,128)} fusion(bf16[4096,2048]{1,0:T(8,128)(2,1)} %all-gather.6.cloned.1.call-done, bf16[4096,1024]{1,0:T(8,128)(2,1)} %bitcast.19), kind=kOutput, calls=%fused_computation | convolution fusion | flops 17179869184 | bytes 33554432 | tf_op jit(solution)/shard_map/dot_general | solution.py:22
  534.9 9.1 %copy.9 = f32[1024,2048]{1,0:T(8,128)} copy(f32[1024,2048]{0,1:T(8,128)} %convolution_bitcast_fusion) | data formatting | bytes 16777216 | tf_op jit(solution)/shard_map/dot_general | solution.py:22
Async XLA Ops:
  6.5 153.5 %copy-start = (bf16[512,2048]{1,0:T(8,128)(2,1)S(1)}, bf16[512,2048]{1,0:T(8,128)(2,1)}, u32[]{:S(2)}) copy-start(bf16[512,2048]{1,0:T(8,128)(2,1)} %param.4) | copy-start | bytes 6291460
  6.5 153.5 %all-gather.4.cloned.1.call-start = ((), (), s32[]{:S(2)}) async-start(), calls=%async_computation.1 | async-start | bytes 10485760 | tf_op jit(solution)/shard_map/all_gather | solution.py:8
  7.3 335.7 %all-gather.8.cloned.1.call-start = ((), (), s32[]{:S(2)}) async-start(), calls=%async_computation.3 | async-start | bytes 10485760 | tf_op jit(solution)/shard_map/all_gather | solution.py:19
  11.3 499.5 %all-gather.6.cloned.1.call-start = ((), (), s32[]{:S(2)}) async-start(), calls=%async_computation.2 | async-start | bytes 18874368 | tf_op jit(solution)/shard_map/all_gather | solution.py:24
  160.0 99.9 %copy-start.1 = (s32[1,512]{1,0:T(1,128)S(1)}, s32[1,512]{1,0:T(1,128)}, u32[]{:S(2)}) copy-start(s32[1,512]{1,0:T(1,128)} %param.7) | copy-start | bytes 6148
Sparse Core Ops, SparseCore 0:
  8.9 151.0 all-gather.3
  161.6 181.3 all-gather.7
  344.8 165.8 all-gather.5
where the time goes:
time: 553 us; the launch traced here: 551 us
  waiting for transfers between devices  233 us (42%)
  blocking collectives  227 us (41%)
  matrix products  53.2 us (10%)
  local copies, waits for them, and re-layouts  24.4 us (4%)
  between operations  13.1 us (2%)
    all_to_all x1, blocking collectives, per_device(): lax.all_to_all(d_full, ('seq', 'tp'), split_axis=1, concat_axis=0, tiled=...  152 us
    all_gather x1, waiting for transfers between devices, per_device(): x_full = lax.all_gather(inputs, 'col', axis=1, tiled=True)  149 us
    all_gather x1, waiting for transfers between devices, per_device(): d_full = lax.all_gather(grads, 'col', axis=1, tiled=True)  78.7 us
    psum x1, blocking collectives, per_device(): whole_sum = lax.psum(partial_squares, 'col')  75 us
    dot_general x1, matrix products, per_device(): lax.dot_general(projected, inputs, (((1,), (1,)), ((), ())), preferred_el...  24.9 us
    dot_general x1, matrix products, per_device(): lax.dot_general(owned_grads, lax.all_gather(products, ('seq', 'tp'), axis...  24.1 us
    all_to_all x1, local copies, waits for them, and re-layouts, per_device(): lax.all_to_all(d_full, ('seq', 'tp'), split_axis=1, concat_axis=0, tiled=...  11.4 us
  transfers between devices with their start and end apart: 3, of which 3 were waited for; matrix products, arithmetic and copies ran while one was open for 8% of the time, Pallas kernels for 0%

commit v1 on v0

v1 whole, which is shorter than its diff:
```python
import functools

import jax
import jax.numpy as jnp
from jax import lax
from jax.experimental import pallas as pl
from jax.experimental.pallas import tpu as pltpu
from jax.sharding import PartitionSpec as P

MESH = pl.DeviceIdType.MESH
MIB = 1 << 20


def gather_kernel(
    n, tps, planes, out_rows,
    x_ref, d_ref, h_ref, seg_ref, segt_ref,
    dr_ref, dc_ref, k_ref,
    xg, dg, hbuf, y, pp, pin, krow,
    x_send, x_recv, d_send, d_recv, c_send, c_recv, a_send, a_recv,
    p_send, p_recv, kz_send, kz_recv, k_send, k_recv, local, h_sem,
):
    rows, cols = x_ref.shape
    width = min(cols, out_rows)
    pieces, per_row_block = cols // width, out_rows // width
    half = planes // 2
    part = rows // n
    tile = min(cols, 256)
    c = lax.axis_index("col")
    p = lax.axis_index("seq") * tps + lax.axis_index("tp")
    parity, mate = lax.rem(p, 2), p + 1 - 2 * lax.rem(p, 2)
    pending = []

    def in_plane(index):
        return {"seq": index // tps, "tp": lax.rem(index, tps)}

    def same_parity(step):
        return 2 * lax.rem(p // 2 + step + half, half) + parity

    def send(make, condition=None):
        if condition is None:
            make().start()
        else:
            pl.when(condition)(lambda: make().start())
        pending.append((make, condition))

    def remote(src, dst, ssem, rsem, to):
        return pltpu.make_async_remote_copy(
            src_ref=src, dst_ref=dst, send_sem=ssem, recv_sem=rsem,
            device_id=to, device_id_type=MESH,
        )

    barrier = pltpu.get_barrier_semaphore()
    for step in range(1, n):
        pl.semaphore_signal(
            barrier, inc=1, device_id={"col": lax.rem(c + step, n)}, device_id_type=MESH
        )
    for step in range(1, planes):
        pl.semaphore_signal(
            barrier, inc=1, device_id=in_plane(lax.rem(p + step, planes)), device_id_type=MESH
        )
    pl.semaphore_wait(barrier, n - 1 + planes - 1)

    def pass_on(src, ring, ssem, rsem, chunk, direction, slot):
        to = c + direction
        ok = (chunk >= 0) & (chunk < n) & (to >= 0) & (to < n)

        def make():
            return remote(src(chunk), ring.at[chunk], ssem.at[slot], rsem.at[chunk], {"col": to})

        send(make, ok)

    def received(ring, ssem, rsem, chunk):
        return remote(ring.at[chunk], ring.at[chunk], ssem.at[0], rsem.at[chunk], {"col": lax.rem(c + 1, n)})

    for side in (0, 1):
        pass_on(lambda chunk: x_ref, xg, x_send, x_recv, c, 1 - 2 * side, side)
    own_x = pltpu.make_async_copy(x_ref, xg.at[c], local.at[0])
    own_x.start()

    def block(ref, index):
        return ref.at[pl.ds(index * rows, rows)]

    own_d = pltpu.make_async_copy(d_ref, block(dc_ref, p), local.at[1])
    own_d.start()
    send(lambda: remote(d_ref, block(dc_ref, p), c_send.at[0], c_recv.at[p], in_plane(mate)))
    for step in range(1, half):
        send(lambda step=step: remote(
            d_ref, block(dc_ref, p), c_send.at[step], c_recv.at[p], in_plane(same_parity(step))
        ))

    def owned(src, chunk, slot):
        for k in range(pieces):
            first = chunk * cols + k * width
            target = first // out_rows
            place = (first - target * out_rows) // width
            ok = (chunk >= 0) & (chunk < n)

            def ends():
                dst = dr_ref.at[
                    pl.ds(p * rows, rows),
                    pl.ds(pl.multiple_of(place * width, width), width),
                ]
                return src(chunk).at[:, pl.ds(k * width, width)], dst, a_recv.at[p, place]

            def make_remote(ends=ends, target=target, k=k):
                s, t, sem = ends()
                return remote(s, t, a_send.at[slot, k], sem, in_plane(target))

            def make_local(ends=ends):
                return pltpu.make_async_copy(*ends())

            send(make_remote, ok & (target != p))
            pl.when(ok & (target == p))(lambda m=make_local: m().start())

    owned(lambda chunk: d_ref, c, 0)

    def work(chunk, wait, first, forward):
        load = pltpu.make_async_copy(
            h_ref.at[pl.ds(pl.multiple_of(chunk * cols, cols), cols)], hbuf, h_sem
        )
        load.start()
        wait()
        forward()
        load.wait()

        @pl.loop(0, cols // tile)
        def _(j):
            at = pl.ds(pl.multiple_of(j * tile, tile), tile)
            term = jnp.dot(xg[chunk], hbuf[:, at], preferred_element_type=jnp.float32)
            y[:, at] = term if first else y[:, at] + term

    work(c, own_x.wait, True, lambda: None)
    for d in range(1, n):
        for side in (0, 1):
            direction = 1 - 2 * side
            chunk = c - direction * d
            ok = (chunk >= 0) & (chunk < n)
            to = c + direction
            slot = 2 * d + side

            def make(chunk=chunk, to=to, slot=slot):
                return remote(xg.at[chunk], xg.at[chunk], x_send.at[slot], x_recv.at[chunk], {"col": to})

            @pl.when(ok)
            def _():
                def forward():
                    if d < n - 1:
                        pl.when((to >= 0) & (to < n))(lambda: make().start())

                work(chunk, lambda: received(xg, x_send, x_recv, chunk).wait_recv(), False, forward)

            if d < n - 1:
                pending.append((make, ok & (to >= 0) & (to < n)))

    for side in (0, 1):
        pass_on(lambda chunk: d_ref, dg, d_send, d_recv, c, 1 - 2 * side, side)

    pp[...] = jnp.zeros_like(pp)

    @pl.loop(0, cols // tile)
    def _(j):
        at = pl.ds(pl.multiple_of(j * tile, tile), tile)
        pp[...] += lax.dot_general(
            y[:, at].astype(jnp.bfloat16), xg[c, :, at],
            (((1,), (1,)), ((), ())), preferred_element_type=jnp.float32,
        )

    def rows_of(ref, index):
        return ref.at[pl.ds(pl.multiple_of(index * part, part), part)]

    for step in range(1, n):
        to = lax.rem(c + step, n)
        send(lambda step=step, to=to: remote(
            rows_of(pp, to), pin.at[c], p_send.at[step], p_recv.at[c], {"col": to}
        ))

    def d_step(d):
        for side in (0, 1):
            direction = 1 - 2 * side
            chunk = c - direction * d
            ok = (chunk >= 0) & (chunk < n)
            pl.when(ok)(lambda: received(dg, d_send, d_recv, chunk).wait_recv())
            if d < n - 1:
                pass_on(lambda ch: dg.at[ch], dg, d_send, d_recv, chunk, direction, 2 * d + side)
            owned(lambda ch: dg.at[ch], chunk, 2 * d + side)

    def c_step():
        for step in range(1, half):
            source = same_parity(-step)
            remote(
                d_ref, block(dc_ref, source), c_send.at[0], c_recv.at[source], in_plane(mate)
            ).wait_recv()
            send(lambda step=step, source=source: remote(
                block(dc_ref, source), block(dc_ref, source),
                c_send.at[half + step], c_recv.at[source], in_plane(mate),
            ))

    def sum_step():
        total = rows_of(pp, c)[...]
        for step in range(1, n):
            source = lax.rem(c - step + n, n)
            remote(
                rows_of(pp, source), pin.at[source], p_send.at[1], p_recv.at[source],
                {"col": source},
            ).wait_recv()
            total = total + pin[source]
        same = rows_of(segt_ref, c)[...] == seg_ref[...]
        krow[...] = jnp.where(same, total, jnp.float32(0.0)).astype(jnp.bfloat16)
        dst = rows_of(k_ref.at[p], c)
        own_k = pltpu.make_async_copy(krow, dst, local.at[2])
        own_k.start()
        for step in range(1, n):
            to = lax.rem(c + step, n)
            send(lambda step=step, to=to: remote(
                krow, rows_of(k_ref.at[p], c), kz_send.at[step], kz_recv.at[c], {"col": to}
            ))
        own_k.wait()

    def square_step():
        for step in range(1, n):
            source = lax.rem(c - step + n, n)
            remote(
                krow, rows_of(k_ref.at[p], source), kz_send.at[1], kz_recv.at[source],
                {"col": source},
            ).wait_recv()
        send(lambda: remote(k_ref.at[p], k_ref.at[p], k_send.at[0], k_recv.at[p], in_plane(mate)))
        for step in range(1, half):
            send(lambda step=step: remote(
                k_ref.at[p], k_ref.at[p], k_send.at[step], k_recv.at[p],
                in_plane(same_parity(step)),
            ))

    def square_relay():
        for step in range(1, half):
            source = same_parity(-step)
            remote(
                k_ref.at[p], k_ref.at[source], k_send.at[0], k_recv.at[source], in_plane(mate)
            ).wait_recv()
            send(lambda step=step, source=source: remote(
                k_ref.at[source], k_ref.at[source],
                k_send.at[half + step], k_recv.at[source], in_plane(mate),
            ))

    c_step()
    stages = [sum_step, square_step, square_relay]
    for d in range(1, max(n, 4)):
        if stages:
            stages.pop(0)()
        if d < n:
            d_step(d)

    for step in range(half):
        other = 2 * lax.rem(p // 2 + step, half) + 1 - parity
        remote(
            d_ref, block(dc_ref, other), c_send.at[0], c_recv.at[other], in_plane(mate)
        ).wait_recv()
        remote(
            k_ref.at[p], k_ref.at[other], k_send.at[0], k_recv.at[other], in_plane(mate)
        ).wait_recv()
    for source in range(planes):
        for place in range(per_row_block):
            dst = dr_ref.at[pl.ds(source * rows, rows), pl.ds(place * width, width)]
            pltpu.make_async_copy(dst, dst, a_recv.at[source, place]).wait()
    own_d.wait()
    for make, condition in pending:
        if condition is None:
            make().wait_send()
        else:
            pl.when(condition)(lambda make=make: make().wait_send())


def product_kernel(k_ref, dc_ref, dr_ref, out_ref, turned):
    step = pl.program_id(0)
    cols = dc_ref.shape[1]
    tile = min(cols, 512)
    turned[...] = dr_ref[...].T

    @pl.when(step == 0)
    def _():
        out_ref[...] = jnp.zeros_like(out_ref)

    @pl.loop(0, cols // tile)
    def _(j):
        at = pl.ds(pl.multiple_of(j * tile, tile), tile)
        z = jnp.dot(k_ref[0], dc_ref[:, at], preferred_element_type=jnp.float32)
        out_ref[:, at] += jnp.dot(
            turned[...], z.astype(jnp.bfloat16), preferred_element_type=jnp.float32
        )


def per_device(n, seqs, tps, inputs, grads, h_in, segments):
    rows, cols = inputs.shape
    planes = seqs * tps
    out_rows = n * cols // planes
    width = min(cols, out_rows)
    part = rows // n
    dma = pltpu.SemaphoreType.DMA
    any_space = pl.BlockSpec(memory_space=pl.ANY)
    vmem = pl.BlockSpec(memory_space=pltpu.VMEM)
    owned_grads, plane_grads, squares = pl.pallas_call(
        functools.partial(gather_kernel, n, tps, planes, out_rows),
        out_shape=(
            jax.ShapeDtypeStruct((planes * rows, out_rows), jnp.bfloat16),
            jax.ShapeDtypeStruct((planes * rows, cols), jnp.bfloat16),
            jax.ShapeDtypeStruct((planes, rows, rows), jnp.bfloat16),
        ),
        in_specs=[any_space, any_space, any_space, vmem, vmem],
        out_specs=(any_space, any_space, any_space),
        scratch_shapes=[
            pltpu.VMEM((n, rows, cols), jnp.bfloat16),
            pltpu.VMEM((n, rows, cols), jnp.bfloat16),
            pltpu.VMEM((cols, cols), jnp.bfloat16),
            pltpu.VMEM((rows, cols), jnp.float32),
            pltpu.VMEM((rows, rows), jnp.float32),
            pltpu.VMEM((n, part, rows), jnp.float32),
            pltpu.VMEM((part, rows), jnp.bfloat16),
            dma((2 * n,)), dma((n,)),
            dma((2 * n,)), dma((n,)),
            dma((planes,)), dma((planes,)),
            dma((2 * n, cols // width)), dma((planes, out_rows // width)),
            dma((n,)), dma((n,)),
            dma((n,)), dma((n,)),
            dma((planes,)), dma((planes,)),
            dma((3,)), dma,
        ],
        compiler_params=pltpu.CompilerParams(
            collective_id=0, has_side_effects=True, vmem_limit_bytes=48 * MIB
        ),
    )(inputs, grads, h_in, segments, segments.reshape(rows, 1))
    return pl.pallas_call(
        product_kernel,
        grid=(planes,),
        out_shape=jax.ShapeDtypeStruct((out_rows, cols), jnp.float32),
        in_specs=[
            pl.BlockSpec((1, rows, rows), lambda s: (s, 0, 0)),
            pl.BlockSpec((rows, cols), lambda s: (s, 0)),
            pl.BlockSpec((rows, out_rows), lambda s: (s, 0)),
        ],
        out_specs=pl.BlockSpec((out_rows, cols), lambda s: (0, 0)),
        scratch_shapes=[pltpu.VMEM((out_rows, rows), jnp.bfloat16)],
        compiler_params=pltpu.CompilerParams(vmem_limit_bytes=48 * MIB),
    )(squares, plane_grads, owned_grads)


def solution(mesh):
    placed = (
        P(("seq", "tp"), "col"),
        P(("seq", "tp"), "col"),
        P(None, "col"),
        P(("seq", "tp"), None),
    )
    sizes = (mesh.shape["col"], mesh.shape["seq"], mesh.shape["tp"])
    return jax.shard_map(
        functools.partial(per_device, *sizes),
        mesh=mesh, in_specs=placed, out_specs=P(("seq", "tp"), "col"), check_vma=False,
    )
```

time: 553 us -> 448 us (0.81)
  Pallas kernels: 0 us -> 441 us
  waiting for transfers between devices: 233 us -> 0 us
  blocking collectives: 227 us -> 0 us
  matrix products: 53.2 us -> 0 us
  local copies, waits for them, and re-layouts: 24.4 us -> 6.86 us
  between operations: 13.1 us -> 0.04 us
    pallas_call x0 -> x2, Pallas kernels: none -> 441 us  [the longest x1 398 us: per_device(): pl.pallas_call(functools.partial(gather_kernel, n, tps, planes, out_rows)...]
    all_gather x3 -> x0, waiting for transfers between devices: 232 us -> none  [the longest x1 149 us: per_device(): x_full = lax.all_gather(inputs, 'col', axis=1, tiled=True)]
    all_to_all x1 -> x0, blocking collectives: 152 us -> none  [per_device(): lax.all_to_all(d_full, ('seq', 'tp'), split_axis=1, concat_axis=0, tiled=...]
    psum x1 -> x0, blocking collectives: 75 us -> none  [per_device(): whole_sum = lax.psum(partial_squares, 'col')]
    dot_general x3 -> x0, matrix products: 53.2 us -> none  [the longest x1 24.9 us: per_device(): lax.dot_general(projected, inputs, (((1,), (1,)), ((), ())), preferred_el...]
    all_to_all x1 -> x0, local copies, waits for them, and re-layouts: 11.4 us -> none  [per_device(): lax.all_to_all(d_full, ('seq', 'tp'), split_axis=1, concat_axis=0, tiled=...]
    dot_general x1 -> x0, local copies, waits for them, and re-layouts: 9.12 us -> none  [per_device(): lax.dot_general(owned_grads, lax.all_gather(products, ('seq', 'tp'), axis...]
  transfers between devices with their start and end apart: 3 -> 0, of which waited for: 3 -> 0; matrix products, arithmetic and copies ran while one was open for 8% -> 0% of each run, Pallas kernels for 0% -> 0%
where the time goes in v1:
time: 448 us
  Pallas kernels  441 us (98%)
  local copies, waits for them, and re-layouts  6.86 us (2%)
    pallas_call x1, Pallas kernels, per_device(): pl.pallas_call(functools.partial(gather_kernel, n, tps, planes, out_rows)...  398 us
    pallas_call x1, Pallas kernels, per_device(): pl.pallas_call(product_kernel, grid=(planes,), out_shape=jax.ShapeDtypeSt...  42.3 us

profile of v1, /device:TPU:7, one launch (start us, length us, event | category | flops | bytes accessed | tf_op | source)
XLA Modules:
  0.0 447.7 jit_solution(821331979624493719)
XLA Ops:
  0.0 0.8 copy.5.segt_ref
  0.8 0.0 copy-start.1
  0.8 1.6 copy-done.1
  2.4 0.0 copy-start.2
  2.4 1.6 copy-done.2
  4.0 0.0 copy-start.3
  4.0 0.7 copy-done.3
  4.7 398.5 %shard_map.46 = (bf16[4096,1024]{1,0:T(8,128)(2,1)}, bf16[4096,2048]{1,0:T(8,128)(2,1)}, bf16[8,512,512]{2,1,0:T(8,128)(2,1)}) custom-call(bf16[512,2048]{1,0:T(8,128)(2,1)S(1)} %copy-done.1, bf16[512,2048]{1,0:T(8,128)(2,1)S(1)} %copy-done.2, bf16[8192,2048]{1,0:T(8,128)(2,1)} %h_ref.1, s32[1,512]{1,0:T(1,128)S(1)} %copy-done.3, s32[512,1]{1,0:T(8,128)S(1)} %copy.5.segt_ref), custom_call_target="tpu_custom_call" | custom-call | tf_op jit(solution)/shard_map/pallas_call | solution.py:300
  403.2 0.0 copy-start
  403.2 2.2 copy-done
  405.4 42.3 %shard_map.47 = f32[1024,2048]{1,0:T(8,128)} custom-call(bf16[8,512,512]{2,1,0:T(8,128)(2,1)S(1)} %copy-done, bf16[4096,2048]{1,0:T(8,128)(2,1)} %get-tuple-element.9.dc_ref, bf16[4096,1024]{1,0:T(8,128)(2,1)} %get-tuple-element.10.dr_ref), custom_call_target="tpu_custom_call" | custom-call | tf_op jit(solution)/shard_map/pallas_call | solution.py:330
Async XLA Ops:
  0.8 1.6 copy-start.1
  2.4 1.6 copy-start.2
  4.0 0.7 copy-start.3
  403.2 2.2 copy-start

commit v2 on v1

--- a/solution.py
+++ b/solution.py
@@ -12,18 +12,18 @@
 
 
 def gather_kernel(
-    n, tps, planes, out_rows,
+    n, tps, planes, out_rows, slabs,
     x_ref, d_ref, h_ref, seg_ref, segt_ref,
-    dr_ref, dc_ref, k_ref,
-    xg, dg, hbuf, y, pp, pin, krow,
+    dr_ref, dc_ref, k_ref, z_ref,
+    xg, dg, hbuf, y, pp, pin, krow, dbuf, kbuf, zbuf,
     x_send, x_recv, d_send, d_recv, c_send, c_recv, a_send, a_recv,
-    p_send, p_recv, kz_send, kz_recv, k_send, k_recv, local, h_sem,
+    p_send, p_recv, kz_send, kz_recv, k_send, k_recv, local, h_sem, z_sem,
 ):
     rows, cols = x_ref.shape
     width = min(cols, out_rows)
     pieces, per_row_block = cols // width, out_rows // width
     half = planes // 2
-    part = rows // n
+    part, slab = rows // n, rows // slabs
     tile = min(cols, 256)
     c = lax.axis_index("col")
     p = lax.axis_index("seq") * tps + lax.axis_index("tp")
@@ -60,20 +60,11 @@
         )
     pl.semaphore_wait(barrier, n - 1 + planes - 1)
 
-    def pass_on(src, ring, ssem, rsem, chunk, direction, slot):
-        to = c + direction
-        ok = (chunk >= 0) & (chunk < n) & (to >= 0) & (to < n)
-
-        def make():
-            return remote(src(chunk), ring.at[chunk], ssem.at[slot], rsem.at[chunk], {"col": to})
-
-        send(make, ok)
-
-    def received(ring, ssem, rsem, chunk):
-        return remote(ring.at[chunk], ring.at[chunk], ssem.at[0], rsem.at[chunk], {"col": lax.rem(c + 1, n)})
-
     for side in (0, 1):
-        pass_on(lambda chunk: x_ref, xg, x_send, x_recv, c, 1 - 2 * side, side)
+        def make(side=side):
+            return remote(x_ref, xg.at[c], x_send.at[side], x_recv.at[c], {"col": c + 1 - 2 * side})
+
+        send(make, (c > 0) if side else (c + 1 < n))
     own_x = pltpu.make_async_copy(x_ref, xg.at[c], local.at[0])
     own_x.start()
 
@@ -88,23 +79,34 @@
             d_ref, block(dc_ref, p), c_send.at[step], c_recv.at[p], in_plane(same_parity(step))
         ))
 
-    def owned(src, chunk, slot):
+    def slab_of(ref, i):
+        return ref.at[pl.ds(i * slab, slab)]
+
+    def pass_on(src, chunk, direction, slot, i):
+        to = c + direction
+        ok = (chunk >= 0) & (chunk < n) & (to >= 0) & (to < n)
+        send(lambda: remote(
+            slab_of(src(chunk), i), slab_of(dg.at[chunk], i),
+            d_send.at[slot, i], d_recv.at[chunk, i], {"col": to},
+        ), ok)
+
+    def owned(src, chunk, slot, i):
         for k in range(pieces):
             first = chunk * cols + k * width
             target = first // out_rows
             place = (first - target * out_rows) // width
             ok = (chunk >= 0) & (chunk < n)
 
-            def ends():
+            def ends(k=k, place=place):
                 dst = dr_ref.at[
-                    pl.ds(p * rows, rows),
+                    pl.ds(p * rows + i * slab, slab),
                     pl.ds(pl.multiple_of(place * width, width), width),
                 ]
-                return src(chunk).at[:, pl.ds(k * width, width)], dst, a_recv.at[p, place]
+                return slab_of(src(chunk), i).at[:, pl.ds(k * width, width)], dst, a_recv.at[p, place]
 
             def make_remote(ends=ends, target=target, k=k):
                 s, t, sem = ends()
-                return remote(s, t, a_send.at[slot, k], sem, in_plane(target))
+                return remote(s, t, a_send.at[slot, i * pieces + k], sem, in_plane(target))
 
             def make_local(ends=ends):
                 return pltpu.make_async_copy(*ends())
@@ -112,7 +114,13 @@
             send(make_remote, ok & (target != p))
             pl.when(ok & (target == p))(lambda m=make_local: m().start())
 
-    owned(lambda chunk: d_ref, c, 0)
+    for i in range(slabs):
+        owned(lambda chunk: d_ref, c, 0, i)
+
+    def received(chunk):
+        return remote(
+            xg.at[chunk], xg.at[chunk], x_send.at[0], x_recv.at[chunk], {"col": lax.rem(c + 1, n)}
+        )
 
     def work(chunk, wait, first, forward):
         load = pltpu.make_async_copy(
@@ -147,13 +155,16 @@
                     if d < n - 1:
                         pl.when((to >= 0) & (to < n))(lambda: make().start())
 
-                work(chunk, lambda: received(xg, x_send, x_recv, chunk).wait_recv(), False, forward)
+                work(chunk, lambda: received(chunk).wait_recv(), False, forward)
 
             if d < n - 1:
                 pending.append((make, ok & (to >= 0) & (to < n)))
 
-    for side in (0, 1):
-        pass_on(lambda chunk: d_ref, dg, d_send, d_recv, c, 1 - 2 * side, side)
+    def own_slab(i):
+        for side in (0, 1):
+            pass_on(lambda chunk: d_ref, c, 1 - 2 * side, side, i)
+
+    own_slab(0)
 
     pp[...] = jnp.zeros_like(pp)
 
@@ -174,17 +185,28 @@
             rows_of(pp, to), pin.at[c], p_send.at[step], p_recv.at[c], {"col": to}
         ))
 
-    def d_step(d):
+    for i in range(1, min(2, slabs)):
+        own_slab(i)
+
+    def d_step(d, i):
         for side in (0, 1):
             direction = 1 - 2 * side
             chunk = c - direction * d
             ok = (chunk >= 0) & (chunk < n)
-            pl.when(ok)(lambda: received(dg, d_send, d_recv, chunk).wait_recv())
+
+            def arrived(chunk=chunk):
+                return remote(
+                    slab_of(dg.at[chunk], i), slab_of(dg.at[chunk], i),
+                    d_send.at[0, i], d_recv.at[chunk, i], {"col": lax.rem(c + 1, n)},
+                )
+
+            pl.when(ok)(lambda arrived=arrived: arrived().wait_recv())
             if d < n - 1:
-                pass_on(lambda ch: dg.at[ch], dg, d_send, d_recv, chunk, direction, 2 * d + side)
-            owned(lambda ch: dg.at[ch], chunk, 2 * d + side)
+                pass_on(lambda ch: dg.at[ch], chunk, direction, 2 * d + side, i)
+            owned(lambda ch: dg.at[ch], chunk, 2 * d + side, i)
 
     def c_step():
+        own_d.wait()
         for step in range(1, half):
             source = same_parity(-step)
             remote(
@@ -241,27 +263,54 @@
                 k_send.at[half + step], k_recv.at[source], in_plane(mate),
             ))
 
+    def z_step(source, arrive):
+        if arrive:
+            remote(
+                d_ref, block(dc_ref, source), c_send.at[0], c_recv.at[source], in_plane(mate)
+            ).wait_recv()
+            remote(
+                k_ref.at[p], k_ref.at[source], k_send.at[0], k_recv.at[source], in_plane(mate)
+            ).wait_recv()
+        loads = (
+            pltpu.make_async_copy(block(dc_ref, source), dbuf, z_sem.at[0]),
+            pltpu.make_async_copy(k_ref.at[source], kbuf, z_sem.at[1]),
+        )
+        for load in loads:
+            load.start()
+        for load in loads:
+            load.wait()
+
+        @pl.loop(0, cols // tile)
+        def _(j):
+            at = pl.ds(pl.multiple_of(j * tile, tile), tile)
+            z = jnp.dot(kbuf[...], dbuf[:, at], preferred_element_type=jnp.float32)
+            zbuf[:, at] = z.astype(jnp.bfloat16)
+
+        store = pltpu.make_async_copy(zbuf, block(z_ref, source), z_sem.at[2])
+        store.start()
+        store.wait()
+
     c_step()
     stages = [sum_step, square_step, square_relay]
-    for d in range(1, max(n, 4)):
-        if stages:
-            stages.pop(0)()
-        if d < n:
-            d_step(d)
-
+    for step in range(half):
+        stages.append(lambda step=step: z_step(same_parity(step), False))
     for step in range(half):
         other = 2 * lax.rem(p // 2 + step, half) + 1 - parity
-        remote(
-            d_ref, block(dc_ref, other), c_send.at[0], c_recv.at[other], in_plane(mate)
-        ).wait_recv()
-        remote(
-            k_ref.at[p], k_ref.at[other], k_send.at[0], k_recv.at[other], in_plane(mate)
-        ).wait_recv()
+        stages.append(lambda other=other: z_step(other, True))
+    for i in range(slabs):
+        for d in range(1, n):
+            if stages:
+                stages.pop(0)()
+            d_step(d, i)
+            if d == 1 and i + 2 < slabs:
+                own_slab(i + 2)
+    for stage in stages:
+        stage()
+
     for source in range(planes):
         for place in range(per_row_block):
             dst = dr_ref.at[pl.ds(source * rows, rows), pl.ds(place * width, width)]
             pltpu.make_async_copy(dst, dst, a_recv.at[source, place]).wait()
-    own_d.wait()
     for make, condition in pending:
         if condition is None:
             make().wait_send()
@@ -269,23 +318,21 @@
             pl.when(condition)(lambda make=make: make().wait_send())
 
 
-def product_kernel(k_ref, dc_ref, dr_ref, out_ref, turned):
-    step = pl.program_id(0)
-    cols = dc_ref.shape[1]
-    tile = min(cols, 512)
-    turned[...] = dr_ref[...].T
-
-    @pl.when(step == 0)
+def product_kernel(z_ref, dr_ref, out_ref, turned):
+    tokens, out_rows = dr_ref.shape
+    deep, high = min(tokens, 512), min(out_rows, 256)
+
+    @pl.when(pl.program_id(0) == 0)
     def _():
-        out_ref[...] = jnp.zeros_like(out_ref)
-
-    @pl.loop(0, cols // tile)
+        @pl.loop(0, tokens // deep)
+        def _(j):
+            at = pl.ds(pl.multiple_of(j * deep, deep), deep)
+            turned[:, at] = dr_ref[at, :].T
+
+    @pl.loop(0, out_rows // high)
     def _(j):
-        at = pl.ds(pl.multiple_of(j * tile, tile), tile)
-        z = jnp.dot(k_ref[0], dc_ref[:, at], preferred_element_type=jnp.float32)
-        out_ref[:, at] += jnp.dot(
-            turned[...], z.astype(jnp.bfloat16), preferred_element_type=jnp.float32
-        )
+        at = pl.ds(pl.multiple_of(j * high, high), high)
+        out_ref[at, :] = jnp.dot(turned[at, :], z_ref[...], preferred_element_type=jnp.float32)
 
 
 def per_device(n, seqs, tps, inputs, grads, h_in, segments):
@@ -294,18 +341,21 @@
     out_rows = n * cols // planes
     width = min(cols, out_rows)
     part = rows // n
+    slabs = 4
+    tokens, tile = planes * rows, min(cols, 256)
     dma = pltpu.SemaphoreType.DMA
     any_space = pl.BlockSpec(memory_space=pl.ANY)
     vmem = pl.BlockSpec(memory_space=pltpu.VMEM)
-    owned_grads, plane_grads, squares = pl.pallas_call(
-        functools.partial(gather_kernel, n, tps, planes, out_rows),
+    owned_grads, _, _, products = pl.pallas_call(
+        functools.partial(gather_kernel, n, tps, planes, out_rows, slabs),
         out_shape=(
             jax.ShapeDtypeStruct((planes * rows, out_rows), jnp.bfloat16),
             jax.ShapeDtypeStruct((planes * rows, cols), jnp.bfloat16),
             jax.ShapeDtypeStruct((planes, rows, rows), jnp.bfloat16),
+            jax.ShapeDtypeStruct((tokens, cols), jnp.bfloat16),
         ),
         in_specs=[any_space, any_space, any_space, vmem, vmem],
-        out_specs=(any_space, any_space, any_space),
+        out_specs=(any_space,) * 4,
         scratch_shapes=[
             pltpu.VMEM((n, rows, cols), jnp.bfloat16),
             pltpu.VMEM((n, rows, cols), jnp.bfloat16),
@@ -314,14 +364,17 @@
             pltpu.VMEM((rows, rows), jnp.float32),
             pltpu.VMEM((n, part, rows), jnp.float32),
             pltpu.VMEM((part, rows), jnp.bfloat16),
+            pltpu.VMEM((rows, cols), jnp.bfloat16),
+            pltpu.VMEM((rows, rows), jnp.bfloat16),
+            pltpu.VMEM((rows, cols), jnp.bfloat16),
             dma((2 * n,)), dma((n,)),
-            dma((2 * n,)), dma((n,)),
+            dma((2 * n, slabs)), dma((n, slabs)),
             dma((planes,)), dma((planes,)),
-            dma((2 * n, cols // width)), dma((planes, out_rows // width)),
+            dma((2 * n, slabs * (cols // width))), dma((planes, out_rows // width)),
             dma((n,)), dma((n,)),
             dma((n,)), dma((n,)),
             dma((planes,)), dma((planes,)),
-            dma((3,)), dma,
+            dma((3,)), dma, dma((3,)),
         ],
         compiler_params=pltpu.CompilerParams(
             collective_id=0, has_side_effects=True, vmem_limit_bytes=48 * MIB
@@ -329,17 +382,16 @@
     )(inputs, grads, h_in, segments, segments.reshape(rows, 1))
     return pl.pallas_call(
         product_kernel,
-        grid=(planes,),
+        grid=(cols // tile,),
         out_shape=jax.ShapeDtypeStruct((out_rows, cols), jnp.float32),
         in_specs=[
-            pl.BlockSpec((1, rows, rows), lambda s: (s, 0, 0)),
-            pl.BlockSpec((rows, cols), lambda s: (s, 0)),
-            pl.BlockSpec((rows, out_rows), lambda s: (s, 0)),
+            pl.BlockSpec((tokens, tile), lambda j: (0, j)),
+            pl.BlockSpec((tokens, out_rows), lambda j: (0, 0)),
         ],
-        out_specs=pl.BlockSpec((out_rows, cols), lambda s: (0, 0)),
-        scratch_shapes=[pltpu.VMEM((out_rows, rows), jnp.bfloat16)],
+        out_specs=pl.BlockSpec((out_rows, tile), lambda j: (0, j)),
+        scratch_shapes=[pltpu.VMEM((out_rows, tokens), jnp.bfloat16)],
         compiler_params=pltpu.CompilerParams(vmem_limit_bytes=48 * MIB),
-    )(squares, plane_grads, owned_grads)
+    )(products, owned_grads)
 
 
 def solution(mesh):

time: 448 us -> 364 us (0.81)
  Pallas kernels: 441 us -> 359 us
    pallas_call x2, Pallas kernels: 441 us -> 359 us  [the longest x1 328 us: per_device(): pl.pallas_call(functools.partial(gather_kernel, n, tps, planes, out_rows,...]
where the time goes in v2:
time: 364 us; the launch traced here: 363 us
  Pallas kernels  359 us (99%)
  local copies, waits for them, and re-layouts  4.68 us (1%)
    pallas_call x1, Pallas kernels, per_device(): pl.pallas_call(functools.partial(gather_kernel, n, tps, planes, out_rows,...  328 us
    pallas_call x1, Pallas kernels, per_device(): pl.pallas_call(product_kernel, grid=(cols // tile,), out_shape=jax.ShapeD...  30.6 us

profile of v2, /device:TPU:7, one launch (start us, length us, event | category | flops | bytes accessed | tf_op | source)
XLA Modules:
  0.0 363.5 jit_solution(4988346246800480929)
XLA Ops:
  0.0 0.8 copy.5.segt_ref
  0.8 0.0 copy-start
  0.8 1.6 copy-done
  2.4 0.0 copy-start.1
  2.4 1.6 copy-done.1
  4.0 0.0 copy-start.2
  4.0 0.7 copy-done.2
  4.7 328.1 %shard_map.46 = (bf16[4096,1024]{1,0:T(8,128)(2,1)}, bf16[4096,2048]{1,0:T(8,128)(2,1)}, bf16[8,512,512]{2,1,0:T(8,128)(2,1)}, bf16[4096,2048]{1,0:T(8,128)(2,1)}) custom-call(bf16[512,2048]{1,0:T(8,128)(2,1)S(1)} %copy-done, bf16[512,2048]{1,0:T(8,128)(2,1)S(1)} %copy-done.1, bf16[8192,2048]{1,0:T(8,128)(2,1)} %h_ref.1, s32[1,512]{1,0:T(1,128)S(1)} %copy-done.2, ...), custom_call_target="tpu_custom_call" | custom-call | tf_op jit(solution)/shard_map/pallas_call | solution.py:349
  332.8 30.6 %shard_map.47 = f32[1024,2048]{1,0:T(8,128)} custom-call(bf16[4096,2048]{1,0:T(8,128)(2,1)} %get-tuple-element.7.z_ref, bf16[4096,1024]{1,0:T(8,128)(2,1)} %get-tuple-element.8.dr_ref), custom_call_target="tpu_custom_call" | custom-call | tf_op jit(solution)/shard_map/pallas_call | solution.py:383
Async XLA Ops:
  0.8 1.6 copy-start
  2.4 1.6 copy-start.1
  4.0 0.7 copy-start.2

commit v3 on v2

--- a/solution.py
+++ b/solution.py
@@ -14,10 +14,11 @@
 def gather_kernel(
     n, tps, planes, out_rows, slabs,
     x_ref, d_ref, h_ref, seg_ref, segt_ref,
-    dr_ref, dc_ref, k_ref, z_ref,
+    dr_ref, dc_ref, k_ref, z_ref, h2_ref,
     xg, dg, hbuf, y, pp, pin, krow, dbuf, kbuf, zbuf,
     x_send, x_recv, d_send, d_recv, c_send, c_recv, a_send, a_recv,
     p_send, p_recv, kz_send, kz_recv, k_send, k_recv, local, h_sem, z_sem,
+    e_send, e_recv, f_send, f_recv,
 ):
     rows, cols = x_ref.shape
     width = min(cols, out_rows)
@@ -29,6 +30,11 @@
     p = lax.axis_index("seq") * tps + lax.axis_index("tp")
     parity, mate = lax.rem(p, 2), p + 1 - 2 * lax.rem(p, 2)
     pending = []
+    share = cols // planes
+    is_edge = (c == 0) | (c == n - 1)
+    is_inner = (c == 1) | (c == n - 2)
+    inner = 1 + (c // (n - 1)) * (n - 3)
+    edge = (n - 1) * (c // (n - 2))
 
     def in_plane(index):
         return {"seq": index // tps, "tp": lax.rem(index, tps)}
@@ -64,9 +70,45 @@
         def make(side=side):
             return remote(x_ref, xg.at[c], x_send.at[side], x_recv.at[c], {"col": c + 1 - 2 * side})
 
-        send(make, (c > 0) if side else (c + 1 < n))
+        send(make, (c > 1) if side else (c + 2 < n))
     own_x = pltpu.make_async_copy(x_ref, xg.at[c], local.at[0])
     own_x.start()
+
+    def h_share(ref, index, chunk=0):
+        return ref.at[pl.ds(pl.multiple_of(chunk * cols + index * share, share), share)]
+
+    send(lambda: remote(
+        h_share(h_ref, p, inner), h_share(h2_ref, p), e_send, e_recv, {"col": inner}
+    ), is_edge)
+
+    def h_fan_out():
+        @pl.when(is_inner)
+        def _():
+            remote(h_share(h2_ref, p), h_share(h2_ref, p), e_send, e_recv, {"col": edge}).wait_recv()
+
+        send(lambda: remote(
+            h_share(h2_ref, p), h_share(h2_ref, p), f_send.at[0], f_recv.at[p], in_plane(mate)
+        ), is_inner)
+        for step in range(1, half):
+            send(lambda step=step: remote(
+                h_share(h2_ref, p), h_share(h2_ref, p), f_send.at[step], f_recv.at[p],
+                in_plane(same_parity(step)),
+            ), is_inner)
+
+    def h_arrived(source):
+        remote(
+            h_share(h2_ref, source), h_share(h2_ref, source), f_send.at[0], f_recv.at[source],
+            in_plane(mate),
+        ).wait_recv()
+
+    def h_relay():
+        for step in range(1, half):
+            source = same_parity(-step)
+            pl.when(is_inner)(lambda source=source: h_arrived(source))
+            send(lambda step=step, source=source: remote(
+                h_share(h2_ref, source), h_share(h2_ref, source),
+                f_send.at[half + step], f_recv.at[source], in_plane(mate),
+            ), is_inner)
 
     def block(ref, index):
         return ref.at[pl.ds(index * rows, rows)]
@@ -82,9 +124,9 @@
     def slab_of(ref, i):
         return ref.at[pl.ds(i * slab, slab)]
 
-    def pass_on(src, chunk, direction, slot, i):
+    def pass_on(src, chunk, direction, slot, i, also=True):
         to = c + direction
-        ok = (chunk >= 0) & (chunk < n) & (to >= 0) & (to < n)
+        ok = (chunk >= 0) & (chunk < n) & (to >= 0) & (to < n) & also
         send(lambda: remote(
             slab_of(src(chunk), i), slab_of(dg.at[chunk], i),
             d_send.at[slot, i], d_recv.at[chunk, i], {"col": to},
@@ -137,12 +179,25 @@
             term = jnp.dot(xg[chunk], hbuf[:, at], preferred_element_type=jnp.float32)
             y[:, at] = term if first else y[:, at] + term
 
+    ahead = min(2, slabs)
+
+    def own_slab(i, side, also=True):
+        pass_on(lambda chunk: d_ref, c, 1 - 2 * side, side, i, also)
+
+    def own_ahead(d):
+        for side in (0, 1):
+            for i in range(ahead):
+                own_slab(i, side, (c == n - 1 - d) if side else (c == d))
+
+    own_ahead(0)
     work(c, own_x.wait, True, lambda: None)
     for d in range(1, n):
         for side in (0, 1):
             direction = 1 - 2 * side
             chunk = c - direction * d
             ok = (chunk >= 0) & (chunk < n)
+            if d == 1:
+                ok = ok & jnp.logical_not(is_edge)
             to = c + direction
             slot = 2 * d + side
 
@@ -159,22 +214,40 @@
 
             if d < n - 1:
                 pending.append((make, ok & (to >= 0) & (to < n)))
-
-    def own_slab(i):
-        for side in (0, 1):
-            pass_on(lambda chunk: d_ref, c, 1 - 2 * side, side, i)
-
-    own_slab(0)
+        if d < n - 1:
+            own_ahead(d)
+        if d == 1:
+            h_fan_out()
+        if d == 2:
+            h_relay()
 
     pp[...] = jnp.zeros_like(pp)
 
-    @pl.loop(0, cols // tile)
-    def _(j):
-        at = pl.ds(pl.multiple_of(j * tile, tile), tile)
-        pp[...] += lax.dot_general(
-            y[:, at].astype(jnp.bfloat16), xg[c, :, at],
-            (((1,), (1,)), ((), ())), preferred_element_type=jnp.float32,
-        )
+    def add_squares(chunk):
+        @pl.loop(0, cols // tile)
+        def _(j):
+            at = pl.ds(pl.multiple_of(j * tile, tile), tile)
+            pp[...] += lax.dot_general(
+                y[:, at].astype(jnp.bfloat16), xg[chunk, :, at],
+                (((1,), (1,)), ((), ())), preferred_element_type=jnp.float32,
+            )
+
+    add_squares(c)
+
+    @pl.when(is_inner)
+    def _():
+        for step in range(half):
+            h_arrived(2 * lax.rem(p // 2 + step, half) + 1 - parity)
+        load = pltpu.make_async_copy(h2_ref, hbuf, h_sem)
+        load.start()
+        load.wait()
+
+        @pl.loop(0, cols // tile)
+        def _(j):
+            at = pl.ds(pl.multiple_of(j * tile, tile), tile)
+            y[:, at] = jnp.dot(xg[c], hbuf[:, at], preferred_element_type=jnp.float32)
+
+        add_squares(edge)
 
     def rows_of(ref, index):
         return ref.at[pl.ds(pl.multiple_of(index * part, part), part)]
@@ -184,9 +257,6 @@
         send(lambda step=step, to=to: remote(
             rows_of(pp, to), pin.at[c], p_send.at[step], p_recv.at[c], {"col": to}
         ))
-
-    for i in range(1, min(2, slabs)):
-        own_slab(i)
 
     def d_step(d, i):
         for side in (0, 1):
@@ -302,8 +372,9 @@
             if stages:
                 stages.pop(0)()
             d_step(d, i)
-            if d == 1 and i + 2 < slabs:
-                own_slab(i + 2)
+            if d == 1 and i + ahead < slabs:
+                own_slab(i + ahead, 0)
+                own_slab(i + ahead, 1)
     for stage in stages:
         stage()
 
@@ -346,16 +417,17 @@
     dma = pltpu.SemaphoreType.DMA
     any_space = pl.BlockSpec(memory_space=pl.ANY)
     vmem = pl.BlockSpec(memory_space=pltpu.VMEM)
-    owned_grads, _, _, products = pl.pallas_call(
+    owned_grads, _, _, products, _ = pl.pallas_call(
         functools.partial(gather_kernel, n, tps, planes, out_rows, slabs),
         out_shape=(
             jax.ShapeDtypeStruct((planes * rows, out_rows), jnp.bfloat16),
             jax.ShapeDtypeStruct((planes * rows, cols), jnp.bfloat16),
             jax.ShapeDtypeStruct((planes, rows, rows), jnp.bfloat16),
             jax.ShapeDtypeStruct((tokens, cols), jnp.bfloat16),
+            jax.ShapeDtypeStruct((cols, cols), jnp.bfloat16),
         ),
         in_specs=[any_space, any_space, any_space, vmem, vmem],
-        out_specs=(any_space,) * 4,
+        out_specs=(any_space,) * 5,
         scratch_shapes=[
             pltpu.VMEM((n, rows, cols), jnp.bfloat16),
             pltpu.VMEM((n, rows, cols), jnp.bfloat16),
@@ -375,6 +447,7 @@
             dma((n,)), dma((n,)),
             dma((planes,)), dma((planes,)),
             dma((3,)), dma, dma((3,)),
+            dma, dma, dma((planes,)), dma((planes,)),
         ],
         compiler_params=pltpu.CompilerParams(
             collective_id=0, has_side_effects=True, vmem_limit_bytes=48 * MIB

time: 364 us -> 437 us (1.20)
  Pallas kernels: 359 us -> 432 us
    pallas_call x1, Pallas kernels: 328 us -> 401 us  [per_device(): pl.pallas_call(functools.partial(gather_kernel, n, tps, planes, out_rows,...]
where the time goes in v3:
time: 437 us; the launch traced here: 436 us
  Pallas kernels  432 us (99%)
  local copies, waits for them, and re-layouts  4.68 us (1%)
    pallas_call x1, Pallas kernels, per_device(): pl.pallas_call(functools.partial(gather_kernel, n, tps, planes, out_rows,...  401 us
    pallas_call x1, Pallas kernels, per_device(): pl.pallas_call(product_kernel, grid=(cols // tile,), out_shape=jax.ShapeD...  30.6 us

profile of v3, /device:TPU:7, one launch (start us, length us, event | category | flops | bytes accessed | tf_op | source)
XLA Modules:
  0.0 436.3 jit_solution(5923886424704155810)
XLA Ops:
  0.0 0.8 copy.5.segt_ref
  0.8 0.0 copy-start
  0.8 1.6 copy-done
  2.4 0.0 copy-start.1
  2.4 1.6 copy-done.1
  4.0 0.0 copy-start.2
  4.0 0.7 copy-done.2
  4.7 401.0 %shard_map.46 = (bf16[4096,1024]{1,0:T(8,128)(2,1)}, bf16[4096,2048]{1,0:T(8,128)(2,1)}, bf16[8,512,512]{2,1,0:T(8,128)(2,1)}, bf16[4096,2048]{1,0:T(8,128)(2,1)}, bf16[2048,2048]{1,0:T(8,128)(2,1)}) custom-call(bf16[512,2048]{1,0:T(8,128)(2,1)S(1)} %copy-done, bf16[512,2048]{1,0:T(8,128)(2,1)S(1)} %copy-done.1, bf16[8192,2048]{1,0:T(8,128)(2,1)} %h_ref.1, ...), custom_call_target="tpu_custom_call" | custom-call | tf_op jit(solution)/shard_map/pallas_call | solution.py:420
  405.7 30.6 %shard_map.47 = f32[1024,2048]{1,0:T(8,128)} custom-call(bf16[4096,2048]{1,0:T(8,128)(2,1)} %get-tuple-element.7.z_ref, bf16[4096,1024]{1,0:T(8,128)(2,1)} %get-tuple-element.8.dr_ref), custom_call_target="tpu_custom_call" | custom-call | tf_op jit(solution)/shard_map/pallas_call | solution.py:456
Async XLA Ops:
  0.8 1.6 copy-start
  2.4 1.6 copy-start.1
  4.0 0.7 copy-start.2

commit v4 on v2

--- a/solution.py
+++ b/solution.py
@@ -82,9 +82,9 @@
     def slab_of(ref, i):
         return ref.at[pl.ds(i * slab, slab)]
 
-    def pass_on(src, chunk, direction, slot, i):
+    def pass_on(src, chunk, direction, slot, i, also=True):
         to = c + direction
-        ok = (chunk >= 0) & (chunk < n) & (to >= 0) & (to < n)
+        ok = (chunk >= 0) & (chunk < n) & (to >= 0) & (to < n) & also
         send(lambda: remote(
             slab_of(src(chunk), i), slab_of(dg.at[chunk], i),
             d_send.at[slot, i], d_recv.at[chunk, i], {"col": to},
@@ -137,6 +137,17 @@
             term = jnp.dot(xg[chunk], hbuf[:, at], preferred_element_type=jnp.float32)
             y[:, at] = term if first else y[:, at] + term
 
+    ahead = min(2, slabs)
+
+    def own_slab(i, side, also=True):
+        pass_on(lambda chunk: d_ref, c, 1 - 2 * side, side, i, also)
+
+    def own_ahead(d):
+        for side in (0, 1):
+            for i in range(ahead):
+                own_slab(i, side, (c == n - 1 - d) if side else (c == d))
+
+    own_ahead(0)
     work(c, own_x.wait, True, lambda: None)
     for d in range(1, n):
         for side in (0, 1):
@@ -159,12 +170,8 @@
 
             if d < n - 1:
                 pending.append((make, ok & (to >= 0) & (to < n)))
-
-    def own_slab(i):
-        for side in (0, 1):
-            pass_on(lambda chunk: d_ref, c, 1 - 2 * side, side, i)
-
-    own_slab(0)
+        if d < n - 1:
+            own_ahead(d)
 
     pp[...] = jnp.zeros_like(pp)
 
@@ -184,9 +191,6 @@
         send(lambda step=step, to=to: remote(
             rows_of(pp, to), pin.at[c], p_send.at[step], p_recv.at[c], {"col": to}
         ))
-
-    for i in range(1, min(2, slabs)):
-        own_slab(i)
 
     def d_step(d, i):
         for side in (0, 1):
@@ -290,8 +294,7 @@
         store.start()
         store.wait()
 
-    c_step()
-    stages = [sum_step, square_step, square_relay]
+    stages = [sum_step, square_step, c_step, square_relay]
     for step in range(half):
         stages.append(lambda step=step: z_step(same_parity(step), False))
     for step in range(half):
@@ -302,8 +305,9 @@
             if stages:
                 stages.pop(0)()
             d_step(d, i)
-            if d == 1 and i + 2 < slabs:
-                own_slab(i + 2)
+            if d == 1 and i + ahead < slabs:
+                own_slab(i + ahead, 0)
+                own_slab(i + ahead, 1)
     for stage in stages:
         stage()
 

time: 364 us -> 365 us (level)
  no operation moved by 1% of the time
where the time goes in v4:
time: 365 us; the launch traced here: 364 us
  Pallas kernels  360 us (99%)
  local copies, waits for them, and re-layouts  4.68 us (1%)
    pallas_call x1, Pallas kernels, per_device(): pl.pallas_call(functools.partial(gather_kernel, n, tps, planes, out_rows,...  329 us
    pallas_call x1, Pallas kernels, per_device(): pl.pallas_call(product_kernel, grid=(cols // tile,), out_shape=jax.ShapeD...  30.6 us

profile of v4, /device:TPU:7, one launch (start us, length us, event | category | flops | bytes accessed | tf_op | source)
XLA Modules:
  0.0 364.3 jit_solution(10091248098777066225)
XLA Ops:
  0.0 0.8 copy.5.segt_ref
  0.8 0.0 copy-start
  0.8 1.6 copy-done
  2.4 0.0 copy-start.1
  2.4 1.6 copy-done.1
  4.0 0.0 copy-start.2
  4.0 0.7 copy-done.2
  4.7 328.9 %shard_map.46 = (bf16[4096,1024]{1,0:T(8,128)(2,1)}, bf16[4096,2048]{1,0:T(8,128)(2,1)}, bf16[8,512,512]{2,1,0:T(8,128)(2,1)}, bf16[4096,2048]{1,0:T(8,128)(2,1)}) custom-call(bf16[512,2048]{1,0:T(8,128)(2,1)S(1)} %copy-done, bf16[512,2048]{1,0:T(8,128)(2,1)S(1)} %copy-done.1, bf16[8192,2048]{1,0:T(8,128)(2,1)} %h_ref.1, s32[1,512]{1,0:T(1,128)S(1)} %copy-done.2, ...), custom_call_target="tpu_custom_call" | custom-call | tf_op jit(solution)/shard_map/pallas_call | solution.py:353
  333.6 30.6 %shard_map.47 = f32[1024,2048]{1,0:T(8,128)} custom-call(bf16[4096,2048]{1,0:T(8,128)(2,1)} %get-tuple-element.7.z_ref, bf16[4096,1024]{1,0:T(8,128)(2,1)} %get-tuple-element.8.dr_ref), custom_call_target="tpu_custom_call" | custom-call | tf_op jit(solution)/shard_map/pallas_call | solution.py:387
Async XLA Ops:
  0.8 1.6 copy-start
  2.4 1.6 copy-start.1
  4.0 0.7 copy-start.2
